TPU v7x, 512 devices: a whole 4x8x8 slice. The times are simulated.
512 devices in a mesh: box: 128 (over z_hi, y, x), freq: 4 (over z_lo, core).
Axes of the slice: x: 4, y: 8, z: 8 (z_hi: 4, z_lo: 2; z = z_hi * 2 + z_lo), core: 2. Of those that a mesh axis runs over, the one named last changes fastest.
Arguments:
- currents: bfloat16 [4, 512, 2, 65536], P(None, 'freq', None, 'box'), may hold values from -6 to 6
- near_kernel: bfloat16 [4, 2, 98304, 512], P('freq', None, 'box'), may hold values from -0.15625 to 0.15625
- project_basis: bfloat16 [4, 2, 65536, 128], P('freq', None, 'box'), may hold values from -0.1875 to 0.1875
- level_self: bfloat16 [7, 4, 2, 16384, 128], P(None, 'freq', None, 'box'), may hold values from -0.25 to 0.25
- level_partner: bfloat16 [7, 4, 2, 16384, 128], P(None, 'freq', None, 'box'), may hold values from -0.25 to 0.25
- expand_basis: bfloat16 [4, 2, 16384, 512], P('freq', None, 'box'), may hold values from -0.375 to 0.375
Outputs:
- voltages: bfloat16 [4, 512, 2, 65536], P(None, 'freq', None, 'box')
All inputs are finite; a program needn't handle non-finite values.
Results may differ from a plain program's by a relative error of at most 0.015.
Values may be sent and summed in bfloat16 or wider, within the bound.
A program may use at most 64 MiB of HBM per device.

v0:
```python
import jax
import jax.numpy as jnp
from jax import lax
from jax.sharding import PartitionSpec as P

HALO = 128


def with_halo(block, sides, width):
    for axis, dim in sides:
        count = lax.axis_size(axis)
        forward = [(i, i + 1) for i in range(count - 1)]
        backward = [(target, source) for source, target in forward]
        low = lax.ppermute(
            lax.slice_in_dim(block, block.shape[dim] - width, None, axis=dim), axis, forward
        )
        high = lax.ppermute(lax.slice_in_dim(block, 0, width, axis=dim), axis, backward)
        block = jnp.concatenate([low, block, high], axis=dim)
    return block


def partner_2(block, axis, stride):
    count = lax.axis_size(axis)
    route = []
    for low in range(count):
        high = low | 1 << stride
        if high != low and high < count:
            route += [(low, high), (high, low)]
    return lax.ppermute(block, axis, route)


def complex_block(real_part, imag_part):
    top_rows = jnp.concatenate([real_part, imag_part], axis=-1)
    bottom_rows = jnp.concatenate([-imag_part, real_part], axis=-1)
    return jnp.concatenate([top_rows, bottom_rows], axis=-2)


def local(currents, near_kernel, project_basis, level_self, level_partner, expand_basis):
    spectra = lax.all_to_all(currents, "freq", split_axis=0, concat_axis=1, tiled=True)
    near_local, project_local, expand_local = (near_kernel, project_basis, expand_basis)
    self_local, partner_local = (level_self, level_partner)
    bin_count = spectra.shape[0]
    scenarios = spectra.shape[1]
    port_count = spectra.shape[3]
    flattened_rows = spectra.reshape(bin_count, scenarios, 2 * port_count)
    project_inward = complex_block(project_local[:, 0], project_local[:, 1])
    series_weights = jnp.einsum(
        "hgx,hxm->hgm", flattened_rows, project_inward, preferred_element_type=jnp.float32
    ).astype(jnp.bfloat16)
    level_total = lax.axis_size("box").bit_length() - 1
    for level_index in range(level_total):
        partner = partner_2(series_weights, "box", level_index)
        own_block = complex_block(self_local[level_index, :, 0], self_local[level_index, :, 1])
        other_block = complex_block(
            partner_local[level_index, :, 0], partner_local[level_index, :, 1]
        )
        mixing_matrix = jnp.concatenate([own_block, other_block], axis=1)
        merged_parts = jnp.concatenate([series_weights, partner], axis=-1)
        series_weights = jnp.einsum(
            "hgx,hxm->hgm", merged_parts, mixing_matrix, preferred_element_type=jnp.float32
        ).astype(jnp.bfloat16)
    expand_outward = complex_block(expand_local[:, 0], expand_local[:, 1])
    distant_field = jnp.einsum(
        "hld,hdp->hlp", series_weights, expand_outward, preferred_element_type=jnp.float32
    )
    with_rims = with_halo(spectra, (("box", 3),), HALO)
    kernel_block = complex_block(near_local[:, 0], near_local[:, 1])
    near_field = jnp.einsum(
        "fsk,fkn->fsn",
        with_rims.reshape(bin_count, scenarios, -1),
        kernel_block,
        preferred_element_type=jnp.float32,
    )
    voltage = (
        (distant_field + near_field)
        .astype(jnp.bfloat16)
        .reshape(bin_count, scenarios, 2, port_count)
    )
    return lax.all_to_all(voltage, "freq", split_axis=1, concat_axis=0, tiled=True)


def solution(mesh):
    return jax.shard_map(
        local,
        mesh=mesh,
        in_specs=(
            P(None, "freq", None, "box"),
            P("freq", None, "box", None),
            P("freq", None, "box", None),
            P(None, "freq", None, "box", None),
            P(None, "freq", None, "box", None),
            P("freq", None, "box", None),
        ),
        out_specs=P(None, "freq", None, "box"),
        check_vma=False,
    )
```

profile of v0, /device:TPU:56, one launch (start us, length us, event | category | flops | bytes accessed | tf_op | source)
XLA Modules:
  0.0 157.1 jit_solution(9558841166506996738)
XLA Ops:
  0.0 3.8 %all-to-all-start = ((bf16[4,128,2,512]{3,2,1,0:T(2,128)(2,1)}), bf16[4,128,2,512]{3,2,1,0:T(2,128)(2,1)S(1)}, u32[]{:S(2)}, u32[]{:S(2)}) async-start(bf16[4,128,2,512]{3,2,1,0:T(2,128)(2,1)} %param.6), calls=%async_computation | async-start | bytes 2097152 | tf_op jit(solution)/shard_map/all_to_all | solution.py:39
  3.9 14.4 %all-to-all-done = bf16[4,128,2,512]{3,2,1,0:T(2,128)(2,1)S(1)} async-done(((bf16[4,128,2,512]{3,2,1,0:T(2,128)(2,1)}), bf16[4,128,2,512]{3,2,1,0:T(2,128)(2,1)S(1)}, u32[]{:S(2)}, u32[]{:S(2)}) %all-to-all-start) | async-done | bytes 1048608 | tf_op jit(solution)/shard_map/all_to_all | solution.py:39
  19.0 3.4 %collective-permute-start = (bf16[1,512,256]{1,2,0:T(8,128)(2,1)S(1)}, bf16[1,512,256]{1,2,0:T(8,128)(2,1)S(1)}, u32[]{:S(2)}, u32[]{:S(2)}) collective-permute-start(bf16[1,512,256]{1,2,0:T(8,128)(2,1)S(1)} %fusion.13), channel_id=1, source_target_pairs={{0,4},{4,0},{8,12},{12,8},{16,20},{20,16},{24,28},{28,24},{32,36},... | collective-permute-start | bytes 786440 | tf_op jit(solution)/shard_map/ppermute | solution.py:29
  22.5 6.0 %collective-permute-done = bf16[1,512,256]{1,2,0:T(8,128)(2,1)S(1)} collective-permute-done((bf16[1,512,256]{1,2,0:T(8,128)(2,1)S(1)}, bf16[1,512,256]{1,2,0:T(8,128)(2,1)S(1)}, u32[]{:S(2)}, u32[]{:S(2)}) %collective-permute-start) | collective-permute-done | bytes 262176 | tf_op jit(solution)/shard_map/ppermute | solution.py:29
  28.9 5.1 %collective-permute-start.1 = (bf16[1,512,256]{1,2,0:T(8,128)(2,1)S(1)}, bf16[1,512,256]{1,2,0:T(8,128)(2,1)S(1)}, u32[]{:S(2)}, u32[]{:S(2)}) collective-permute-start(bf16[1,512,256]{1,2,0:T(8,128)(2,1)S(1)} %fusion.7), channel_id=1, source_target_pairs={{0,8},{8,0},{4,12},{12,4},{16,24},{24,16},{20,28},{28,20},{32,40},... | collective-permute-start | bytes 786440 | tf_op jit(solution)/shard_map/ppermute | solution.py:29
  34.0 5.1 %collective-permute-done.1 = bf16[1,512,256]{1,2,0:T(8,128)(2,1)S(1)} collective-permute-done((bf16[1,512,256]{1,2,0:T(8,128)(2,1)S(1)}, bf16[1,512,256]{1,2,0:T(8,128)(2,1)S(1)}, u32[]{:S(2)}, u32[]{:S(2)}) %collective-permute-start.1) | collective-permute-done | bytes 262176 | tf_op jit(solution)/shard_map/ppermute | solution.py:29
  39.4 3.3 %collective-permute-start.2 = (bf16[1,512,256]{1,2,0:T(8,128)(2,1)S(1)}, bf16[1,512,256]{1,2,0:T(8,128)(2,1)S(1)}, u32[]{:S(2)}, u32[]{:S(2)}) collective-permute-start(bf16[1,512,256]{1,2,0:T(8,128)(2,1)S(1)} %fusion.8), channel_id=1, source_target_pairs={{0,16},{16,0},{4,20},{20,4},{8,24},{24,8},{12,28},{28,12},{32,48},... | collective-permute-start | bytes 786440 | tf_op jit(solution)/shard_map/ppermute | solution.py:29
  42.8 4.9 %collective-permute-done.2 = bf16[1,512,256]{1,2,0:T(8,128)(2,1)S(1)} collective-permute-done((bf16[1,512,256]{1,2,0:T(8,128)(2,1)S(1)}, bf16[1,512,256]{1,2,0:T(8,128)(2,1)S(1)}, u32[]{:S(2)}, u32[]{:S(2)}) %collective-permute-start.2) | collective-permute-done | bytes 262176 | tf_op jit(solution)/shard_map/ppermute | solution.py:29
  48.1 4.0 %collective-permute-start.3 = (bf16[1,512,256]{1,2,0:T(8,128)(2,1)S(1)}, bf16[1,512,256]{1,2,0:T(8,128)(2,1)S(1)}, u32[]{:S(2)}, u32[]{:S(2)}) collective-permute-start(bf16[1,512,256]{1,2,0:T(8,128)(2,1)S(1)} %fusion.9), channel_id=1, source_target_pairs={{0,32},{32,0},{4,36},{36,4},{8,40},{40,8},{12,44},{44,12},{16,48},... | collective-permute-start | bytes 786440 | tf_op jit(solution)/shard_map/ppermute | solution.py:29
  52.2 8.9 %collective-permute-done.3 = bf16[1,512,256]{1,2,0:T(8,128)(2,1)S(1)} collective-permute-done((bf16[1,512,256]{1,2,0:T(8,128)(2,1)S(1)}, bf16[1,512,256]{1,2,0:T(8,128)(2,1)S(1)}, u32[]{:S(2)}, u32[]{:S(2)}) %collective-permute-start.3) | collective-permute-done | bytes 262176 | tf_op jit(solution)/shard_map/ppermute | solution.py:29
  61.4 7.1 %collective-permute-start.4 = (bf16[1,512,256]{1,2,0:T(8,128)(2,1)S(1)}, bf16[1,512,256]{1,2,0:T(8,128)(2,1)S(1)}, u32[]{:S(2)}, u32[]{:S(2)}) collective-permute-start(bf16[1,512,256]{1,2,0:T(8,128)(2,1)S(1)} %fusion.10), channel_id=1, source_target_pairs={{0,64},{64,0},{4,68},{68,4},{8,72},{72,8},{12,76},{76,12},{16,80},... | collective-permute-start | bytes 786440 | tf_op jit(solution)/shard_map/ppermute | solution.py:29
  68.9 3.3 %collective-permute-start.7 = (bf16[1,512,2,128]{3,2,1,0:T(2,128)(2,1)S(1)}, bf16[1,512,2,128]{3,2,1,0:T(2,128)(2,1)S(1)}, u32[]{:S(2)}, u32[]{:S(2)}) collective-permute-start(bf16[1,512,2,128]{3,2,1,0:T(2,128)(2,1)S(1)} %get-tuple-element.7), channel_id=1, source_target_pairs={{0,4},{4,8},{8,12},{12,16},{16,20},{20,24},{24,28},{28,32},{32,36}... | collective-permute-start | bytes 786440 | tf_op jit(solution)/shard_map/ppermute | solution.py:14
  72.2 4.6 %collective-permute-start.8 = (bf16[1,512,2,128]{3,2,1,0:T(2,128)(2,1)S(1)}, bf16[1,512,2,128]{3,2,1,0:T(2,128)(2,1)S(1)}, u32[]{:S(2)}, u32[]{:S(2)}) collective-permute-start(bf16[1,512,2,128]{3,2,1,0:T(2,128)(2,1)S(1)} %get-tuple-element.8), channel_id=1, source_target_pairs={{4,0},{8,4},{12,8},{16,12},{20,16},{24,20},{28,24},{32,28},{36,32}... | collective-permute-start | bytes 786440 | tf_op jit(solution)/shard_map/ppermute | solution.py:17
  76.9 3.4 %collective-permute-done.4 = bf16[1,512,256]{1,2,0:T(8,128)(2,1)S(1)} collective-permute-done((bf16[1,512,256]{1,2,0:T(8,128)(2,1)S(1)}, bf16[1,512,256]{1,2,0:T(8,128)(2,1)S(1)}, u32[]{:S(2)}, u32[]{:S(2)}) %collective-permute-start.4) | collective-permute-done | bytes 262176 | tf_op jit(solution)/shard_map/ppermute | solution.py:29
  80.6 4.6 %collective-permute-start.5 = (bf16[1,512,256]{1,2,0:T(8,128)(2,1)S(1)}, bf16[1,512,256]{1,2,0:T(8,128)(2,1)S(1)}, u32[]{:S(2)}, u32[]{:S(2)}) collective-permute-start(bf16[1,512,256]{1,2,0:T(8,128)(2,1)S(1)} %fusion.11), channel_id=1, source_target_pairs={{0,128},{128,0},{4,132},{132,4},{8,136},{136,8},{12,140},{140,12},... | collective-permute-start | bytes 786440 | tf_op jit(solution)/shard_map/ppermute | solution.py:29
  85.2 2.0 %collective-permute-done.7 = bf16[1,512,2,128]{3,2,1,0:T(2,128)(2,1)S(1)} collective-permute-done((bf16[1,512,2,128]{3,2,1,0:T(2,128)(2,1)S(1)}, bf16[1,512,2,128]{3,2,1,0:T(2,128)(2,1)S(1)}, u32[]{:S(2)}, u32[]{:S(2)}) %collective-permute-start.7) | collective-permute-done | bytes 262176 | tf_op jit(solution)/shard_map/ppermute | solution.py:14
  87.2 1.5 pad_maximum_fusion
  89.0 15.8 %collective-permute-done.5 = bf16[1,512,256]{1,2,0:T(8,128)(2,1)S(1)} collective-permute-done((bf16[1,512,256]{1,2,0:T(8,128)(2,1)S(1)}, bf16[1,512,256]{1,2,0:T(8,128)(2,1)S(1)}, u32[]{:S(2)}, u32[]{:S(2)}) %collective-permute-start.5) | collective-permute-done | bytes 262176 | tf_op jit(solution)/shard_map/ppermute | solution.py:29
  105.2 16.8 %collective-permute-start.6 = (bf16[1,512,256]{1,2,0:T(8,128)(2,1)S(1)}, bf16[1,512,256]{1,2,0:T(8,128)(2,1)S(1)}, u32[]{:S(2)}, u32[]{:S(2)}) collective-permute-start(bf16[1,512,256]{1,2,0:T(8,128)(2,1)S(1)} %fusion.12), channel_id=1, source_target_pairs={{0,256},{256,0},{4,260},{260,4},{8,264},{264,8},{12,268},{268,12},... | collective-permute-start | bytes 786440 | tf_op jit(solution)/shard_map/ppermute | solution.py:29
  122.0 14.0 %fusion = f32[512,1024]{1,0:T(8,128)} fusion(bf16[512,1536]{1,0:T(8,128)(2,1)S(1)} %bitcast.188, bf16[1,768,512]{2,1,0:T(8,128)(2,1)S(1)} %get-tuple-element.6, bf16[1,768,512]{2,1,0:T(8,128)(2,1)S(1)} %fusion.180, bf16[1,768,512]{2,1,0:T(8,128)(2,1)S(1)} %get-tuple-element.5), kind=kOutput, calls=%fused_computation.1 | convolution fusion | flops 1623195648 | bytes 6029312 | tf_op jit(solution)/shard_map/fsk,fkn->fsn/dot_general | solution.py:68
  136.0 2.4 %add_convert_fusion = bf16[512,1024]{1,0:T(8,128)(2,1)S(1)} fusion(f32[512,1024]{1,0:T(8,128)} %fusion, bf16[1,512,256]{1,2,0:T(8,128)(2,1)S(1)} %collective-permute-done.6, bf16[1,512,256]{1,2,0:T(8,128)(2,1)S(1)} %fusion.12, bf16[1,128,512]{2,1,0:T(8,128)(2,1)S(1)} %get-tuple-element.52, bf16[1,128,512]{2,1,0:T(8,128)(2,1)S(1)} %fusion.179, ...), kind=kOutput, calls=%fused_computation.8 | convolution fusion | flops 409075712 | bytes 4259840 | tf_op jit(solution)/shard_map/hld,hdp->hlp/dot_general | solution.py:63
  138.4 0.8 reshape.318
  139.2 16.9 %all_to_all.24 = bf16[1,512,2,512]{3,2,0,1:T(2,128)(2,1)S(1)} all-to-all(bf16[1,512,2,512]{3,2,0,1:T(2,128)(2,1)S(1)} %bitcast.186), channel_id=1, replica_groups=mesh['box'=128,'freq'=4] {'freq'}, dimensions={1} | all-to-all | bytes 2097152 | tf_op jit(solution)/shard_map/all_to_all | solution.py:79
  156.1 1.0 copy.11
  (31 shorter events, 3.8 us)
Async XLA Ops:
  0.0 3.8 %copy-start.3 = (bf16[1,2,512,128]{3,2,1,0:T(8,128)(2,1)S(1)}, bf16[1,2,512,128]{3,2,1,0:T(8,128)(2,1)}, u32[]{:S(2)}) copy-start(bf16[1,2,512,128]{3,2,1,0:T(8,128)(2,1)} %param.8) | copy-start | bytes 786436
  0.0 3.8 %copy-start.2 = (bf16[7,1,2,128,128]{4,3,2,1,0:T(8,128)(2,1)S(1)}, bf16[7,1,2,128,128]{4,3,2,1,0:T(8,128)(2,1)}, u32[]{:S(2)}) copy-start(bf16[7,1,2,128,128]{4,3,2,1,0:T(8,128)(2,1)} %param.9) | copy-start | bytes 1376260
  0.0 18.2 %all-to-all-start = ((bf16[4,128,2,512]{3,2,1,0:T(2,128)(2,1)}), bf16[4,128,2,512]{3,2,1,0:T(2,128)(2,1)S(1)}, u32[]{:S(2)}, u32[]{:S(2)}) async-start(bf16[4,128,2,512]{3,2,1,0:T(2,128)(2,1)} %param.6), calls=%async_computation | async-start | bytes 2097152 | tf_op jit(solution)/shard_map/all_to_all | solution.py:39
  18.5 3.9 %copy-start.1 = (bf16[7,1,2,128,128]{4,3,2,1,0:T(8,128)(2,1)S(1)}, bf16[7,1,2,128,128]{4,3,2,1,0:T(8,128)(2,1)}, u32[]{:S(2)}) copy-start(bf16[7,1,2,128,128]{4,3,2,1,0:T(8,128)(2,1)} %param.10) | copy-start | bytes 1376260
  19.0 9.5 %collective-permute-start = (bf16[1,512,256]{1,2,0:T(8,128)(2,1)S(1)}, bf16[1,512,256]{1,2,0:T(8,128)(2,1)S(1)}, u32[]{:S(2)}, u32[]{:S(2)}) collective-permute-start(bf16[1,512,256]{1,2,0:T(8,128)(2,1)S(1)} %fusion.13), channel_id=1, source_target_pairs={{0,4},{4,0},{8,12},{12,8},{16,20},{20,16},{24,28},{28,24},{32,36},... | collective-permute-start | bytes 786440 | tf_op jit(solution)/shard_map/ppermute | solution.py:29
  22.5 11.5 %copy-start.4 = (bf16[1,2,128,512]{3,2,1,0:T(8,128)(2,1)S(1)}, bf16[1,2,128,512]{3,2,1,0:T(8,128)(2,1)}, u32[]{:S(2)}) copy-start(bf16[1,2,128,512]{3,2,1,0:T(8,128)(2,1)} %param.11) | copy-start | bytes 786436
  28.9 13.9 %copy-start = (bf16[1,2,768,512]{3,2,1,0:T(8,128)(2,1)S(1)}, bf16[1,2,768,512]{3,2,1,0:T(8,128)(2,1)}, u32[]{:S(2)}) copy-start(bf16[1,2,768,512]{3,2,1,0:T(8,128)(2,1)} %param.7) | copy-start | bytes 4718596
  28.9 10.2 %collective-permute-start.1 = (bf16[1,512,256]{1,2,0:T(8,128)(2,1)S(1)}, bf16[1,512,256]{1,2,0:T(8,128)(2,1)S(1)}, u32[]{:S(2)}, u32[]{:S(2)}) collective-permute-start(bf16[1,512,256]{1,2,0:T(8,128)(2,1)S(1)} %fusion.7), channel_id=1, source_target_pairs={{0,8},{8,0},{4,12},{12,4},{16,24},{24,16},{20,28},{28,20},{32,40},... | collective-permute-start | bytes 786440 | tf_op jit(solution)/shard_map/ppermute | solution.py:29
  39.4 8.3 %collective-permute-start.2 = (bf16[1,512,256]{1,2,0:T(8,128)(2,1)S(1)}, bf16[1,512,256]{1,2,0:T(8,128)(2,1)S(1)}, u32[]{:S(2)}, u32[]{:S(2)}) collective-permute-start(bf16[1,512,256]{1,2,0:T(8,128)(2,1)S(1)} %fusion.8), channel_id=1, source_target_pairs={{0,16},{16,0},{4,20},{20,4},{8,24},{24,8},{12,28},{28,12},{32,48},... | collective-permute-start | bytes 786440 | tf_op jit(solution)/shard_map/ppermute | solution.py:29
  48.1 13.0 %collective-permute-start.3 = (bf16[1,512,256]{1,2,0:T(8,128)(2,1)S(1)}, bf16[1,512,256]{1,2,0:T(8,128)(2,1)S(1)}, u32[]{:S(2)}, u32[]{:S(2)}) collective-permute-start(bf16[1,512,256]{1,2,0:T(8,128)(2,1)S(1)} %fusion.9), channel_id=1, source_target_pairs={{0,32},{32,0},{4,36},{36,4},{8,40},{40,8},{12,44},{44,12},{16,48},... | collective-permute-start | bytes 786440 | tf_op jit(solution)/shard_map/ppermute | solution.py:29
  61.4 18.9 %collective-permute-start.4 = (bf16[1,512,256]{1,2,0:T(8,128)(2,1)S(1)}, bf16[1,512,256]{1,2,0:T(8,128)(2,1)S(1)}, u32[]{:S(2)}, u32[]{:S(2)}) collective-permute-start(bf16[1,512,256]{1,2,0:T(8,128)(2,1)S(1)} %fusion.10), channel_id=1, source_target_pairs={{0,64},{64,0},{4,68},{68,4},{8,72},{72,8},{12,76},{76,12},{16,80},... | collective-permute-start | bytes 786440 | tf_op jit(solution)/shard_map/ppermute | solution.py:29
  68.9 18.3 %collective-permute-start.7 = (bf16[1,512,2,128]{3,2,1,0:T(2,128)(2,1)S(1)}, bf16[1,512,2,128]{3,2,1,0:T(2,128)(2,1)S(1)}, u32[]{:S(2)}, u32[]{:S(2)}) collective-permute-start(bf16[1,512,2,128]{3,2,1,0:T(2,128)(2,1)S(1)} %get-tuple-element.7), channel_id=1, source_target_pairs={{0,4},{4,8},{8,12},{12,16},{16,20},{20,24},{24,28},{28,32},{32,36}... | collective-permute-start | bytes 786440 | tf_op jit(solution)/shard_map/ppermute | solution.py:14
  72.2 15.0 %collective-permute-start.8 = (bf16[1,512,2,128]{3,2,1,0:T(2,128)(2,1)S(1)}, bf16[1,512,2,128]{3,2,1,0:T(2,128)(2,1)S(1)}, u32[]{:S(2)}, u32[]{:S(2)}) collective-permute-start(bf16[1,512,2,128]{3,2,1,0:T(2,128)(2,1)S(1)} %get-tuple-element.8), channel_id=1, source_target_pairs={{4,0},{8,4},{12,8},{16,12},{20,16},{24,20},{28,24},{32,28},{36,32}... | collective-permute-start | bytes 786440 | tf_op jit(solution)/shard_map/ppermute | solution.py:17
  80.6 24.2 %collective-permute-start.5 = (bf16[1,512,256]{1,2,0:T(8,128)(2,1)S(1)}, bf16[1,512,256]{1,2,0:T(8,128)(2,1)S(1)}, u32[]{:S(2)}, u32[]{:S(2)}) collective-permute-start(bf16[1,512,256]{1,2,0:T(8,128)(2,1)S(1)} %fusion.11), channel_id=1, source_target_pairs={{0,128},{128,0},{4,132},{132,4},{8,136},{136,8},{12,140},{140,12},... | collective-permute-start | bytes 786440 | tf_op jit(solution)/shard_map/ppermute | solution.py:29
  105.2 30.8 %collective-permute-start.6 = (bf16[1,512,256]{1,2,0:T(8,128)(2,1)S(1)}, bf16[1,512,256]{1,2,0:T(8,128)(2,1)S(1)}, u32[]{:S(2)}, u32[]{:S(2)}) collective-permute-start(bf16[1,512,256]{1,2,0:T(8,128)(2,1)S(1)} %fusion.12), channel_id=1, source_target_pairs={{0,256},{256,0},{4,260},{260,4},{8,264},{264,8},{12,268},{268,12},... | collective-permute-start | bytes 786440 | tf_op jit(solution)/shard_map/ppermute | solution.py:29
where the time goes:
time: 158 us; the launch traced here: 157 us
  waiting for transfers between devices  60.5 us (38%)
  starting transfers between devices  55.9 us (35%)
  matrix products  18.9 us (12%)
  blocking collectives  16.9 us (11%)
  local copies, waits for them, and re-layouts  2.86 us (2%)
  other arithmetic  1.7 us (1%)
    ppermute x7, starting transfers between devices, partner_2(): return lax.ppermute(block, axis, route)  44.2 us
    ppermute x7, waiting for transfers between devices, partner_2(): return lax.ppermute(block, axis, route)  44.1 us
    all_to_all x1, blocking collectives, local(): lax.all_to_all(voltage, 'freq', split_axis=1, concat_axis=0, tiled=True)  16.9 us
    all_to_all x1, waiting for transfers between devices, local(): lax.all_to_all(currents, 'freq', split_axis=0, concat_axis=1, tiled=True)  14.4 us
    dot_general x1, matrix products, local(): jnp.einsum('fsk,fkn->fsn', with_rims.reshape(bin_count, scenarios, -1), k...  14 us
    ppermute x1, starting transfers between devices, with_halo(): lax.ppermute(lax.slice_in_dim(block, 0, width, axis=dim), axis, backward)  4.63 us
    all_to_all x1, starting transfers between devices, local(): lax.all_to_all(currents, 'freq', split_axis=0, concat_axis=1, tiled=True)  3.77 us
    ppermute x1, starting transfers between devices, with_halo(): lax.ppermute(lax.slice_in_dim(block, block.shape[dim] - width, None, axis...  3.32 us
  transfers between devices with their start and end apart: 10, of which 8 were waited for; matrix products, arithmetic and copies ran while one was open for 11% of the time, Pallas kernels for 0%

commit v1 on v0

v1 whole, which is shorter than its diff:
```python
import functools

import jax
import jax.numpy as jnp
from jax import lax
from jax.experimental import pallas as pl
from jax.experimental.pallas import tpu as pltpu
from jax.sharding import PartitionSpec as P

HALO = 128
SUB = 2
MESH = pl.DeviceIdType.MESH
STAGES = ((0, 1), (2,), (3, 4), (5, 6))
STEPS = (
    ("project", 0, 0), ("project", 0, 1), ("rims", 0), ("project", 1, 0),
    ("project", 1, 1), ("level", 0, 0, 0), ("rims", 1), ("project", 2, 0),
    ("onward",), ("level", 0, 0, 1), ("project", 3, 0), ("level", 0, 1, 0),
    ("level", 1, 0, 0), ("level", 0, 1, 1), ("level", 1, 0, 1), ("project", 2, 1),
    ("rims", 2), ("level", 0, 2, 0), ("level", 1, 1, 0), ("level", 2, 0, 0),
    ("level", 0, 3, 0), ("project", 3, 1), ("level", 1, 1, 1), ("near", 0),
    ("rims", 3), ("level", 0, 2, 1), ("level", 2, 0, 1), ("level", 0, 3, 1),
    ("level", 1, 2, 0), ("level", 2, 1, 0), ("level", 3, 0, 0), ("near", 1),
    ("level", 1, 3, 0), ("level", 2, 1, 1), ("level", 3, 0, 1), ("level", 1, 2, 1),
    ("level", 2, 2, 0), ("finish", 0, 1), ("finish", 0, 0), ("level", 3, 1, 0),
    ("level", 2, 3, 0), ("level", 1, 3, 1), ("finish", 1, 0), ("level", 2, 2, 1),
    ("level", 3, 2, 0), ("finish", 2, 0), ("level", 2, 3, 1), ("level", 3, 3, 0),
    ("level", 3, 1, 1), ("finish", 3, 0), ("finish", 1, 1), ("level", 3, 2, 1),
    ("finish", 2, 1), ("level", 3, 3, 1), ("finish", 3, 1),
)


def flip(index, stride):
    return index + stride - 2 * stride * ((index // stride) % 2)


def kernel(
    cur, near, proj, own, other, expand, out,
    spec, low_rim, high_rim, near_re, near_im, near_neg, w_in, w_lev, w_out, far_raw, w_far, w_two, coef, part_in, near_sum, volt,
    load_sem, spec_sem, fwd_send, fwd_recv, rim_send, rim_recv, lev_send, lev_recv, far_send, far_recv, ret_send, ret_recv, home_sem,
):
    box, f = lax.axis_index("box"), lax.axis_index("freq")
    boxes = lax.axis_size("box")
    levels = own.shape[0]
    scen, ports = spec.shape[2], spec.shape[3]
    rank = proj.shape[-1]
    rows = scen // SUB
    up, down = lax.rem(box + 1, boxes), lax.rem(box + boxes - 1, boxes)
    peers = [f, flip(f, 1), flip(f, 2), flip(flip(f, 2), 1)]
    stages = len(STAGES)
    mates, pairs = [], []
    for stage in STAGES:
        first = flip(box, 1 << stage[0])
        if len(stage) == 2:
            mates.append([first, flip(box, 1 << stage[1]), flip(first, 1 << stage[1])])
            pairs.append(mates[-1][1])
        else:
            mates.append([first])
    everyone = [there for group in mates for there in group] + [up, down]

    barrier = pltpu.get_barrier_semaphore()
    for slot in (2, 3, 1):
        pl.semaphore_signal(barrier, inc=1, device_id={"freq": peers[slot]}, device_id_type=MESH)
    for there in everyone:
        pl.semaphore_signal(barrier, inc=1, device_id={"box": there}, device_id_type=MESH)

    own_copy = pltpu.make_async_copy(cur.at[f], spec.at[0], spec_sem)
    own_copy.start()
    loads = []

    def load(source, target):
        copy = pltpu.make_async_copy(source, target, load_sem.at[len(loads)])
        copy.start()
        loads.append(copy)

    load(proj.at[0, 0], w_in.at[0:ports, 0:rank])
    load(proj.at[0, 1], w_in.at[0:ports, rank : 2 * rank])
    load(proj.at[0, 0], w_in.at[ports : 2 * ports, rank : 2 * rank])
    for source, base in ((own, 0), (other, 2 * rank)):
        load(source.at[:, 0, 0], w_lev.at[:, base : base + rank, 0:rank])
        load(source.at[:, 0, 1], w_lev.at[:, base : base + rank, rank : 2 * rank])
        load(source.at[:, 0, 0], w_lev.at[:, base + rank : base + 2 * rank, rank : 2 * rank])
    load(near.at[0, 0], near_re)
    load(near.at[0, 1], near_im)
    load(expand.at[0, 0], w_out.at[0:rank, 0:ports])
    load(expand.at[0, 1], w_out.at[0:rank, ports : 2 * ports])
    load(expand.at[0, 0], w_out.at[rank : 2 * rank, ports : 2 * ports])

    pl.semaphore_wait(barrier, 3 + len(everyone))

    def forward(slot, part):
        lines = pl.ds(part * rows, rows)
        return pltpu.make_async_remote_copy(
            src_ref=cur.at[peers[slot], :, lines],
            dst_ref=spec.at[slot, :, lines],
            send_sem=fwd_send.at[slot, part],
            recv_sem=fwd_recv.at[slot, part],
            device_id={"freq": peers[slot]},
            device_id_type=MESH,
        )

    def rim(slot, side):
        columns = pl.ds(ports - HALO, HALO) if side == 0 else pl.ds(0, HALO)
        return pltpu.make_async_remote_copy(
            src_ref=spec.at[slot, :, :, columns],
            dst_ref=(low_rim, high_rim)[side].at[slot],
            send_sem=rim_send.at[side, slot],
            recv_sem=rim_recv.at[side, slot],
            device_id={"box": (up, down)[side]},
            device_id_type=MESH,
        )

    def exchange(stage, slot, part):
        lines = pl.ds(part * rows, rows)
        return [
            pltpu.make_async_remote_copy(
                src_ref=coef.at[stage, slot, lines],
                dst_ref=part_in.at[stage, place, slot, lines],
                send_sem=lev_send.at[stage, place, slot, part],
                recv_sem=lev_recv.at[stage, place, slot, part],
                device_id={"box": there},
                device_id_type=MESH,
            )
            for place, there in enumerate(mates[stage])
        ]

    twos = [stage for stage in range(stages) if len(STAGES[stage]) == 2]

    def factors(place):
        stage = STAGES[twos[place]]
        return [
            pltpu.make_async_remote_copy(
                src_ref=source.at[stage[0], 0],
                dst_ref=far_raw.at[place, which],
                send_sem=far_send.at[place, which],
                recv_sem=far_recv.at[place, which],
                device_id={"box": pairs[place]},
                device_id_type=MESH,
            )
            for which, source in enumerate((own, other))
        ]

    def give_back(slot, part):
        lines = pl.ds(part * rows, rows)
        return pltpu.make_async_remote_copy(
            src_ref=volt.at[slot, :, lines],
            dst_ref=out.at[f, :, lines],
            send_sem=ret_send.at[slot, part],
            recv_sem=ret_recv.at[slot, part],
            device_id={"freq": peers[slot]},
            device_id_type=MESH,
        )

    def arrive(slot, part):
        lines = pl.ds(part * rows, rows)
        return pltpu.make_async_remote_copy(
            src_ref=volt.at[slot, :, lines],
            dst_ref=out.at[peers[slot], :, lines],
            send_sem=ret_send.at[slot, part],
            recv_sem=ret_recv.at[slot, part],
            device_id={"freq": peers[slot]},
            device_id_type=MESH,
        )

    def home(part):
        lines = pl.ds(part * rows, rows)
        return pltpu.make_async_copy(volt.at[0, :, lines], out.at[f, :, lines], home_sem.at[part])

    for slot in (2, 3):
        forward(slot, 0).start()
    for part in range(SUB):
        forward(1, part).start()
    for place in range(len(twos)):
        for copy in factors(place):
            copy.start()

    def dot(left, right):
        return jnp.dot(left, right, preferred_element_type=jnp.float32)

    for copy in loads[:3]:
        copy.wait()
    w_in[ports : 2 * ports, 0:rank] = -w_in[0:ports, rank : 2 * rank]
    own_copy.wait()
    prepared = set()

    def prepare(what):
        if what in prepared:
            return
        prepared.add(what)
        if what == "level":
            for copy in loads[3:9]:
                copy.wait()
            for base in (0, 2 * rank):
                w_lev[:, base + rank : base + 2 * rank, 0:rank] = -w_lev[:, base : base + rank, rank : 2 * rank]
        elif isinstance(what, int):
            for copy in factors(what):
                copy.wait()
            low, high = STAGES[twos[what]]
            for which in range(2):
                top, real, imag = 2 * rank * which, far_raw[what, which, 0], far_raw[what, which, 1]
                w_far[top : top + rank, 0:rank] = real
                w_far[top : top + rank, rank : 2 * rank] = imag
                w_far[top + rank : top + 2 * rank, 0:rank] = -imag
                w_far[top + rank : top + 2 * rank, rank : 2 * rank] = real
            near_half = dot(w_lev[low], w_lev[high, 0 : 2 * rank])
            far_half = dot(w_far[...], w_lev[high, 2 * rank : 4 * rank])
            w_two[what, 0 : 4 * rank] = near_half.astype(jnp.bfloat16)
            w_two[what, 4 * rank : 8 * rank] = far_half.astype(jnp.bfloat16)
        elif what == "near":
            for copy in loads[9:11]:
                copy.wait()

            @pl.when(box == 0)
            def _():
                near_re[0:HALO] = jnp.zeros((HALO, ports), jnp.bfloat16)
                near_im[0:HALO] = jnp.zeros((HALO, ports), jnp.bfloat16)

            @pl.when(box == boxes - 1)
            def _():
                near_re[HALO + ports :] = jnp.zeros((HALO, ports), jnp.bfloat16)
                near_im[HALO + ports :] = jnp.zeros((HALO, ports), jnp.bfloat16)

            near_neg[...] = -near_im[...]
        else:
            for copy in loads[11:14]:
                copy.wait()
            w_out[rank : 2 * rank, 0:ports] = -w_out[0:rank, ports : 2 * ports]

    for step in STEPS:
        kind = step[0]
        if kind == "project":
            slot, part = step[1:]
            lines = pl.ds(part * rows, rows)
            if slot != 0:
                forward(slot, part).wait_recv()
            total = dot(spec[slot, 0, lines], w_in[0:ports]) + dot(spec[slot, 1, lines], w_in[ports : 2 * ports])
            coef[0, slot, lines] = total.astype(jnp.bfloat16)
            for copy in exchange(0, slot, part):
                copy.start()
            prepare("level")
        elif kind == "onward":
            for part in range(1, SUB):
                for slot in (2, 3):
                    forward(slot, part).start()
        elif kind == "rims":
            for side in range(2):
                rim(step[1], side).start()
        elif kind == "level":
            stage, slot, part = step[1:]
            lines = pl.ds(part * rows, rows)
            if stage in twos:
                prepare(twos.index(stage))
                weights = w_two.at[twos.index(stage)]
            else:
                weights = w_lev.at[STAGES[stage][0]]
            for copy in exchange(stage, slot, part):
                copy.wait_recv()
            blocks = [coef[stage, slot, lines]] + [part_in[stage, place, slot, lines] for place in range(len(mates[stage]))]
            total = dot(jnp.concatenate(blocks, axis=-1), weights[...])
            coef[stage + 1, slot, lines] = total.astype(jnp.bfloat16)
            if stage + 1 < stages:
                for copy in exchange(stage + 1, slot, part):
                    copy.start()
        elif kind == "near":
            prepare("near")
            prepare("out")
            pair = (2 * step[1], 2 * step[1] + 1)
            for slot in pair:
                for side in range(2):
                    rim(slot, side).wait_recv()

            def window(component):
                bands = [low_rim[pair[0] : pair[1] + 1, component], spec[pair[0] : pair[1] + 1, component], high_rim[pair[0] : pair[1] + 1, component]]
                return jnp.concatenate([band.reshape(2 * scen, band.shape[-1]) for band in bands], axis=-1)

            real, imag = window(0), window(1)
            near_sum[pair[0] : pair[1] + 1, :, 0:ports] = (dot(real, near_re[...]) + dot(imag, near_neg[...])).reshape(2, scen, ports)
            near_sum[pair[0] : pair[1] + 1, :, ports:] = (dot(real, near_im[...]) + dot(imag, near_re[...])).reshape(2, scen, ports)
        else:
            slot, part = step[1:]
            lines = pl.ds(part * rows, rows)
            total = (dot(coef[stages, slot, lines], w_out[...]) + near_sum[slot, lines]).astype(jnp.bfloat16)
            volt[slot, 0, lines] = total[:, 0:ports]
            volt[slot, 1, lines] = total[:, ports:]
            if slot == 0:
                home(part).start()
            else:
                give_back(slot, part).start()

    for slot in range(4):
        for side in range(2):
            rim(slot, side).wait_send()
        for part in range(SUB):
            for stage in range(stages):
                for copy in exchange(stage, slot, part):
                    copy.wait_send()
            if slot == 0:
                home(part).wait()
            else:
                forward(slot, part).wait_send()
                give_back(slot, part).wait_send()
                arrive(slot, part).wait_recv()


def local(currents, near_kernel, project_basis, level_self, level_partner, expand_basis):
    spectra = jnp.transpose(currents, (0, 2, 1, 3))
    bins, _, scen, ports = spectra.shape
    levels, rank = level_self.shape[0], level_self.shape[-1]
    width = near_kernel.shape[2]
    half = jnp.bfloat16
    stages, twos = len(STAGES), sum(len(stage) == 2 for stage in STAGES)
    voltages = pl.pallas_call(
        kernel,
        out_shape=jax.ShapeDtypeStruct(spectra.shape, half),
        in_specs=[pl.BlockSpec(memory_space=pl.ANY)] * 6,
        out_specs=pl.BlockSpec(memory_space=pl.ANY),
        scratch_shapes=[
            pltpu.VMEM((4, 2, scen, ports), half),
            pltpu.VMEM((4, 2, scen, HALO), half),
            pltpu.VMEM((4, 2, scen, HALO), half),
            pltpu.VMEM((width, ports), half),
            pltpu.VMEM((width, ports), half),
            pltpu.VMEM((width, ports), half),
            pltpu.VMEM((2 * ports, 2 * rank), half),
            pltpu.VMEM((levels, 4 * rank, 2 * rank), half),
            pltpu.VMEM((2 * rank, 2 * ports), half),
            pltpu.VMEM((max(twos, 1), 2, 2, rank, rank), half),
            pltpu.VMEM((4 * rank, 2 * rank), half),
            pltpu.VMEM((max(twos, 1), 8 * rank, 2 * rank), half),
            pltpu.VMEM((stages + 1, 4, scen, 2 * rank), half),
            pltpu.VMEM((stages, 3, 4, scen, 2 * rank), half),
            pltpu.VMEM((4, scen, 2 * ports), jnp.float32),
            pltpu.VMEM((4, 2, scen, ports), half),
            pltpu.SemaphoreType.DMA((14,)),
            pltpu.SemaphoreType.DMA,
            pltpu.SemaphoreType.DMA((4, SUB)),
            pltpu.SemaphoreType.DMA((4, SUB)),
            pltpu.SemaphoreType.DMA((2, 4)),
            pltpu.SemaphoreType.DMA((2, 4)),
            pltpu.SemaphoreType.DMA((stages, 3, 4, SUB)),
            pltpu.SemaphoreType.DMA((stages, 3, 4, SUB)),
            pltpu.SemaphoreType.DMA((max(twos, 1), 2)),
            pltpu.SemaphoreType.DMA((max(twos, 1), 2)),
            pltpu.SemaphoreType.DMA((4, SUB)),
            pltpu.SemaphoreType.DMA((4, SUB)),
            pltpu.SemaphoreType.DMA((SUB,)),
        ],
        compiler_params=pltpu.CompilerParams(collective_id=0, has_side_effects=True, vmem_limit_bytes=50 * 1024 * 1024),
        cost_estimate=pl.CostEstimate(flops=3 << 30, bytes_accessed=6 << 20, transcendentals=0),
    )(spectra, near_kernel, project_basis, level_self, level_partner, expand_basis)
    return jnp.transpose(voltages, (0, 2, 1, 3))


def solution(mesh):
    return jax.shard_map(
        local,
        mesh=mesh,
        in_specs=(
            P(None, "freq", None, "box"),
            P("freq", None, "box", None),
            P("freq", None, "box", None),
            P(None, "freq", None, "box", None),
            P(None, "freq", None, "box", None),
            P("freq", None, "box", None),
        ),
        out_specs=P(None, "freq", None, "box"),
        check_vma=False,
    )
```

time: 158 us -> 84.4 us (0.53)
  the two profiles are of different devices: /device:TPU:56 before, /device:TPU:1 now
where the time goes in v1:
time: 84.4 us; the launch traced here: 83.4 us
  Pallas kernels  79.7 us (94%)
  local copies, waits for them, and re-layouts  3.63 us (4%)
    pallas_call x1, Pallas kernels, local(): pl.pallas_call(kernel, out_shape=jax.ShapeDtypeStruct(spectra.shape, half...  79.7 us
    transpose x1, local copies, waits for them, and re-layouts, local(): return jnp.transpose(voltages, (0, 2, 1, 3))  2.05 us

profile of v1, /device:TPU:1, one launch (start us, length us, event | category | flops | bytes accessed | tf_op | source)
XLA Modules:
  0.0 83.4 jit_solution(16067949550783735982)
XLA Ops:
  0.0 0.0 copy-start.3
  0.0 0.0 copy-start.1
  0.0 0.0 copy-start
  0.0 0.0 copy-start.2
  0.0 1.5 %copy.10 = bf16[4,128,2,512]{3,1,2,0:T(8,128)(2,1)S(1)} copy(bf16[4,128,2,512]{3,2,1,0:T(2,128)(2,1)} %param.6) | data formatting | bytes 2097152 | tf_op args[0]
  1.5 0.0 copy-done.3
  1.5 0.0 copy-done.1
  1.6 0.0 copy-done
  1.6 0.1 copy-done.2
  1.6 79.7 %shard_map.64 = bf16[4,2,128,512]{3,2,1,0:T(8,128)(2,1)S(1)} custom-call(bf16[4,2,128,512]{3,2,1,0:T(8,128)(2,1)S(1)} %bitcast.5, bf16[1,2,768,512]{3,2,1,0:T(8,128)(2,1)} %near.1, bf16[1,2,512,128]{3,2,1,0:T(8,128)(2,1)S(1)} %copy-done.2, bf16[7,1,2,128,128]{4,3,2,1,0:T(8,128)(2,1)S(1)} %copy-done, bf16[7,1,2,128,128]{4,3,2,1,0:T(8,128)(2,1)S(1)} %copy-done.1, ...), custom_call_target="tpu_custom_call" | custom-call | flops 3221225472 | bytes 6291456 | tf_op jit(solution)/shard_map/pallas_call | solution.py:311
  81.3 2.0 %copy.8 = bf16[4,128,2,512]{3,2,1,0:T(2,128)(2,1)} copy(bf16[4,128,2,512]{3,1,2,0:T(8,128)(2,1)S(1)} %bitcast.4) | data formatting | bytes 2097152 | tf_op jit(solution)/shard_map/transpose | solution.py:350
Async XLA Ops:
  0.0 1.5 %copy-start.3 = (bf16[1,2,128,512]{3,2,1,0:T(8,128)(2,1)S(1)}, bf16[1,2,128,512]{3,2,1,0:T(8,128)(2,1)}, u32[]{:S(2)}) copy-start(bf16[1,2,128,512]{3,2,1,0:T(8,128)(2,1)} %expand.1) | copy-start | bytes 786436
  0.0 1.5 %copy-start.1 = (bf16[7,1,2,128,128]{4,3,2,1,0:T(8,128)(2,1)S(1)}, bf16[7,1,2,128,128]{4,3,2,1,0:T(8,128)(2,1)}, u32[]{:S(2)}) copy-start(bf16[7,1,2,128,128]{4,3,2,1,0:T(8,128)(2,1)} %other.1) | copy-start | bytes 1376260
  0.0 1.6 %copy-start = (bf16[7,1,2,128,128]{4,3,2,1,0:T(8,128)(2,1)S(1)}, bf16[7,1,2,128,128]{4,3,2,1,0:T(8,128)(2,1)}, u32[]{:S(2)}) copy-start(bf16[7,1,2,128,128]{4,3,2,1,0:T(8,128)(2,1)} %own.1) | copy-start | bytes 1376260
  0.0 1.6 %copy-start.2 = (bf16[1,2,512,128]{3,2,1,0:T(8,128)(2,1)S(1)}, bf16[1,2,512,128]{3,2,1,0:T(8,128)(2,1)}, u32[]{:S(2)}) copy-start(bf16[1,2,512,128]{3,2,1,0:T(8,128)(2,1)} %proj.1) | copy-start | bytes 786436

commit v2 on v1

--- a/solution.py
+++ b/solution.py
@@ -8,24 +8,18 @@
 from jax.sharding import PartitionSpec as P
 
 HALO = 128
-SUB = 2
+SUB = 1
 MESH = pl.DeviceIdType.MESH
 STAGES = ((0, 1), (2,), (3, 4), (5, 6))
 STEPS = (
-    ("project", 0, 0), ("project", 0, 1), ("rims", 0), ("project", 1, 0),
-    ("project", 1, 1), ("level", 0, 0, 0), ("rims", 1), ("project", 2, 0),
-    ("onward",), ("level", 0, 0, 1), ("project", 3, 0), ("level", 0, 1, 0),
-    ("level", 1, 0, 0), ("level", 0, 1, 1), ("level", 1, 0, 1), ("project", 2, 1),
-    ("rims", 2), ("level", 0, 2, 0), ("level", 1, 1, 0), ("level", 2, 0, 0),
-    ("level", 0, 3, 0), ("project", 3, 1), ("level", 1, 1, 1), ("near", 0),
-    ("rims", 3), ("level", 0, 2, 1), ("level", 2, 0, 1), ("level", 0, 3, 1),
-    ("level", 1, 2, 0), ("level", 2, 1, 0), ("level", 3, 0, 0), ("near", 1),
-    ("level", 1, 3, 0), ("level", 2, 1, 1), ("level", 3, 0, 1), ("level", 1, 2, 1),
-    ("level", 2, 2, 0), ("finish", 0, 1), ("finish", 0, 0), ("level", 3, 1, 0),
-    ("level", 2, 3, 0), ("level", 1, 3, 1), ("finish", 1, 0), ("level", 2, 2, 1),
-    ("level", 3, 2, 0), ("finish", 2, 0), ("level", 2, 3, 1), ("level", 3, 3, 0),
-    ("level", 3, 1, 1), ("finish", 3, 0), ("finish", 1, 1), ("level", 3, 2, 1),
-    ("finish", 2, 1), ("level", 3, 3, 1), ("finish", 3, 1),
+    ("project", 0, 0), ("project", 1, 0), ("rims", 0), ("level", 0, 0, 0),
+    ("rims", 1), ("level", 0, 1, 0), ("project", 2, 0), ("level", 1, 0, 0),
+    ("level", 0, 2, 0), ("project", 3, 0), ("level", 1, 1, 0), ("near", 0),
+    ("level", 2, 0, 0), ("level", 0, 3, 0), ("rims", 2), ("rims", 3),
+    ("level", 1, 2, 0), ("level", 2, 1, 0), ("level", 1, 3, 0), ("near", 1),
+    ("level", 2, 2, 0), ("level", 2, 3, 0), ("level", 3, 2, 0), ("level", 3, 0, 0),
+    ("finish", 2, 0), ("level", 3, 3, 0), ("finish", 3, 0), ("level", 3, 1, 0),
+    ("finish", 0, 0), ("finish", 1, 0),
 )
 
 
@@ -92,7 +86,7 @@
         return pltpu.make_async_remote_copy(
             src_ref=cur.at[peers[slot], :, lines],
             dst_ref=spec.at[slot, :, lines],
-            send_sem=fwd_send.at[slot, part],
+            send_sem=fwd_send.at[slot],
             recv_sem=fwd_recv.at[slot, part],
             device_id={"freq": peers[slot]},
             device_id_type=MESH,
@@ -103,7 +97,7 @@
         return pltpu.make_async_remote_copy(
             src_ref=spec.at[slot, :, :, columns],
             dst_ref=(low_rim, high_rim)[side].at[slot],
-            send_sem=rim_send.at[side, slot],
+            send_sem=rim_send.at[side],
             recv_sem=rim_recv.at[side, slot],
             device_id={"box": (up, down)[side]},
             device_id_type=MESH,
@@ -115,13 +109,20 @@
             pltpu.make_async_remote_copy(
                 src_ref=coef.at[stage, slot, lines],
                 dst_ref=part_in.at[stage, place, slot, lines],
-                send_sem=lev_send.at[stage, place, slot, part],
-                recv_sem=lev_recv.at[stage, place, slot, part],
+                send_sem=lev_send.at[stage, place],
+                recv_sem=lev_recv.at[stage, slot, part],
                 device_id={"box": there},
                 device_id_type=MESH,
             )
             for place, there in enumerate(mates[stage])
         ]
+
+    def landed(stage, slot, part):
+        block = part_in.at[stage, pl.ds(0, len(mates[stage])), slot, pl.ds(part * rows, rows)]
+        return pltpu.make_async_copy(block, block, lev_recv.at[stage, slot, part])
+
+    def drained(ref, sem):
+        pltpu.make_async_copy(ref, ref, sem).wait()
 
     twos = [stage for stage in range(stages) if len(STAGES[stage]) == 2]
 
@@ -144,26 +145,15 @@
         return pltpu.make_async_remote_copy(
             src_ref=volt.at[slot, :, lines],
             dst_ref=out.at[f, :, lines],
-            send_sem=ret_send.at[slot, part],
-            recv_sem=ret_recv.at[slot, part],
+            send_sem=ret_send.at[slot],
+            recv_sem=ret_recv.at[slot],
             device_id={"freq": peers[slot]},
             device_id_type=MESH,
         )
 
-    def arrive(slot, part):
-        lines = pl.ds(part * rows, rows)
-        return pltpu.make_async_remote_copy(
-            src_ref=volt.at[slot, :, lines],
-            dst_ref=out.at[peers[slot], :, lines],
-            send_sem=ret_send.at[slot, part],
-            recv_sem=ret_recv.at[slot, part],
-            device_id={"freq": peers[slot]},
-            device_id_type=MESH,
-        )
-
     def home(part):
         lines = pl.ds(part * rows, rows)
-        return pltpu.make_async_copy(volt.at[0, :, lines], out.at[f, :, lines], home_sem.at[part])
+        return pltpu.make_async_copy(volt.at[0, :, lines], out.at[f, :, lines], home_sem)
 
     for slot in (2, 3):
         forward(slot, 0).start()
@@ -252,8 +242,7 @@
                 weights = w_two.at[twos.index(stage)]
             else:
                 weights = w_lev.at[STAGES[stage][0]]
-            for copy in exchange(stage, slot, part):
-                copy.wait_recv()
+            landed(stage, slot, part).wait()
             blocks = [coef[stage, slot, lines]] + [part_in[stage, place, slot, lines] for place in range(len(mates[stage]))]
             total = dot(jnp.concatenate(blocks, axis=-1), weights[...])
             coef[stage + 1, slot, lines] = total.astype(jnp.bfloat16)
@@ -286,19 +275,16 @@
             else:
                 give_back(slot, part).start()
 
-    for slot in range(4):
-        for side in range(2):
-            rim(slot, side).wait_send()
-        for part in range(SUB):
-            for stage in range(stages):
-                for copy in exchange(stage, slot, part):
-                    copy.wait_send()
-            if slot == 0:
-                home(part).wait()
-            else:
-                forward(slot, part).wait_send()
-                give_back(slot, part).wait_send()
-                arrive(slot, part).wait_recv()
+    drained(low_rim, rim_send.at[0])
+    drained(high_rim, rim_send.at[1])
+    for stage in range(stages):
+        for place in range(len(mates[stage])):
+            drained(coef.at[stage], lev_send.at[stage, place])
+    for slot in range(1, 4):
+        drained(spec.at[slot], fwd_send.at[slot])
+        drained(volt.at[slot], ret_send.at[slot])
+        drained(out.at[peers[slot]], ret_recv.at[slot])
+    drained(volt.at[0], home_sem)
 
 
 def local(currents, near_kernel, project_basis, level_self, level_partner, expand_basis):
@@ -332,17 +318,17 @@
             pltpu.VMEM((4, 2, scen, ports), half),
             pltpu.SemaphoreType.DMA((14,)),
             pltpu.SemaphoreType.DMA,
+            pltpu.SemaphoreType.DMA((4,)),
             pltpu.SemaphoreType.DMA((4, SUB)),
-            pltpu.SemaphoreType.DMA((4, SUB)),
+            pltpu.SemaphoreType.DMA((2,)),
             pltpu.SemaphoreType.DMA((2, 4)),
-            pltpu.SemaphoreType.DMA((2, 4)),
-            pltpu.SemaphoreType.DMA((stages, 3, 4, SUB)),
-            pltpu.SemaphoreType.DMA((stages, 3, 4, SUB)),
+            pltpu.SemaphoreType.DMA((stages, 3)),
+            pltpu.SemaphoreType.DMA((stages, 4, SUB)),
             pltpu.SemaphoreType.DMA((max(twos, 1), 2)),
             pltpu.SemaphoreType.DMA((max(twos, 1), 2)),
-            pltpu.SemaphoreType.DMA((4, SUB)),
-            pltpu.SemaphoreType.DMA((4, SUB)),
-            pltpu.SemaphoreType.DMA((SUB,)),
+            pltpu.SemaphoreType.DMA((4,)),
+            pltpu.SemaphoreType.DMA((4,)),
+            pltpu.SemaphoreType.DMA,
         ],
         compiler_params=pltpu.CompilerParams(collective_id=0, has_side_effects=True, vmem_limit_bytes=50 * 1024 * 1024),
         cost_estimate=pl.CostEstimate(flops=3 << 30, bytes_accessed=6 << 20, transcendentals=0),

time: 84.4 us -> 84 us (level); the launches traced: 83.4 us -> 83.8 us
  no operation moved by 1% of the time
where the time goes in v2:
time: 84 us; the launch traced here: 83.8 us
  Pallas kernels  80.2 us (95%)
  local copies, waits for them, and re-layouts  3.63 us (4%)
    pallas_call x1, Pallas kernels, local(): pl.pallas_call(kernel, out_shape=jax.ShapeDtypeStruct(spectra.shape, half...  80.2 us
    transpose x1, local copies, waits for them, and re-layouts, local(): return jnp.transpose(voltages, (0, 2, 1, 3))  2.05 us

profile of v2, /device:TPU:1, one launch (start us, length us, event | category | flops | bytes accessed | tf_op | source)
XLA Modules:
  0.0 83.8 jit_solution(3607867857978375895)
XLA Ops:
  0.0 0.0 copy-start.3
  0.0 0.0 copy-start.1
  0.0 0.0 copy-start
  0.0 0.0 copy-start.2
  0.0 1.5 %copy.10 = bf16[4,128,2,512]{3,1,2,0:T(8,128)(2,1)S(1)} copy(bf16[4,128,2,512]{3,2,1,0:T(2,128)(2,1)} %param.6) | data formatting | bytes 2097152 | tf_op args[0]
  1.5 0.0 copy-done.3
  1.5 0.0 copy-done.1
  1.6 0.0 copy-done
  1.6 0.1 copy-done.2
  1.6 80.2 %shard_map.64 = bf16[4,2,128,512]{3,2,1,0:T(8,128)(2,1)S(1)} custom-call(bf16[4,2,128,512]{3,2,1,0:T(8,128)(2,1)S(1)} %bitcast.5, bf16[1,2,768,512]{3,2,1,0:T(8,128)(2,1)} %near.1, bf16[1,2,512,128]{3,2,1,0:T(8,128)(2,1)S(1)} %copy-done.2, bf16[7,1,2,128,128]{4,3,2,1,0:T(8,128)(2,1)S(1)} %copy-done, bf16[7,1,2,128,128]{4,3,2,1,0:T(8,128)(2,1)S(1)} %copy-done.1, ...), custom_call_target="tpu_custom_call" | custom-call | flops 3221225472 | bytes 6291456 | tf_op jit(solution)/shard_map/pallas_call | solution.py:297
  81.8 2.0 %copy.8 = bf16[4,128,2,512]{3,2,1,0:T(2,128)(2,1)} copy(bf16[4,128,2,512]{3,1,2,0:T(8,128)(2,1)S(1)} %bitcast.4) | data formatting | bytes 2097152 | tf_op jit(solution)/shard_map/transpose | solution.py:336
Async XLA Ops:
  0.0 1.5 %copy-start.3 = (bf16[1,2,128,512]{3,2,1,0:T(8,128)(2,1)S(1)}, bf16[1,2,128,512]{3,2,1,0:T(8,128)(2,1)}, u32[]{:S(2)}) copy-start(bf16[1,2,128,512]{3,2,1,0:T(8,128)(2,1)} %expand.1) | copy-start | bytes 786436
  0.0 1.5 %copy-start.1 = (bf16[7,1,2,128,128]{4,3,2,1,0:T(8,128)(2,1)S(1)}, bf16[7,1,2,128,128]{4,3,2,1,0:T(8,128)(2,1)}, u32[]{:S(2)}) copy-start(bf16[7,1,2,128,128]{4,3,2,1,0:T(8,128)(2,1)} %other.1) | copy-start | bytes 1376260
  0.0 1.6 %copy-start = (bf16[7,1,2,128,128]{4,3,2,1,0:T(8,128)(2,1)S(1)}, bf16[7,1,2,128,128]{4,3,2,1,0:T(8,128)(2,1)}, u32[]{:S(2)}) copy-start(bf16[7,1,2,128,128]{4,3,2,1,0:T(8,128)(2,1)} %own.1) | copy-start | bytes 1376260
  0.0 1.6 %copy-start.2 = (bf16[1,2,512,128]{3,2,1,0:T(8,128)(2,1)S(1)}, bf16[1,2,512,128]{3,2,1,0:T(8,128)(2,1)}, u32[]{:S(2)}) copy-start(bf16[1,2,512,128]{3,2,1,0:T(8,128)(2,1)} %proj.1) | copy-start | bytes 786436

commit v3 on v2

--- a/solution.py
+++ b/solution.py
@@ -8,18 +8,26 @@
 from jax.sharding import PartitionSpec as P
 
 HALO = 128
-SUB = 1
+TILE = 256
+SUB = 2
 MESH = pl.DeviceIdType.MESH
 STAGES = ((0, 1), (2,), (3, 4), (5, 6))
 STEPS = (
-    ("project", 0, 0), ("project", 1, 0), ("rims", 0), ("level", 0, 0, 0),
-    ("rims", 1), ("level", 0, 1, 0), ("project", 2, 0), ("level", 1, 0, 0),
-    ("level", 0, 2, 0), ("project", 3, 0), ("level", 1, 1, 0), ("near", 0),
-    ("level", 2, 0, 0), ("level", 0, 3, 0), ("rims", 2), ("rims", 3),
-    ("level", 1, 2, 0), ("level", 2, 1, 0), ("level", 1, 3, 0), ("near", 1),
-    ("level", 2, 2, 0), ("level", 2, 3, 0), ("level", 3, 2, 0), ("level", 3, 0, 0),
-    ("finish", 2, 0), ("level", 3, 3, 0), ("finish", 3, 0), ("level", 3, 1, 0),
-    ("finish", 0, 0), ("finish", 1, 0),
+    ("project", 0, 0), ("project", 0, 1), ("rims", 0), ("project", 1, 0),
+    ("onward",), ("project", 1, 1), ("level", 0, 0, 0), ("project", 2, 0),
+    ("rims", 1), ("level", 0, 0, 1), ("level", 0, 1, 0), ("level", 1, 0, 0),
+    ("project", 3, 0), ("level", 1, 0, 1), ("project", 2, 1), ("level", 0, 1, 1),
+    ("near", 0), ("rims", 2), ("level", 1, 1, 0), ("near", 1),
+    ("project", 3, 1), ("level", 0, 2, 0), ("level", 0, 3, 0), ("rims", 3),
+    ("level", 0, 2, 1), ("level", 2, 0, 0), ("level", 1, 1, 1), ("near", 2),
+    ("level", 0, 3, 1), ("level", 2, 0, 1), ("level", 1, 2, 0), ("level", 2, 1, 0),
+    ("level", 3, 0, 0), ("level", 1, 3, 0), ("level", 2, 1, 1), ("finish", 0, 0),
+    ("level", 1, 2, 1), ("level", 2, 2, 0), ("level", 3, 1, 0), ("level", 2, 3, 0),
+    ("finish", 1, 0), ("level", 1, 3, 1), ("level", 2, 2, 1), ("level", 3, 0, 1),
+    ("level", 3, 2, 0), ("finish", 2, 0), ("level", 3, 1, 1), ("level", 2, 3, 1),
+    ("finish", 0, 1), ("level", 3, 3, 0), ("level", 3, 2, 1), ("finish", 2, 1),
+    ("finish", 1, 1), ("near", 3), ("finish", 3, 0), ("level", 3, 3, 1),
+    ("finish", 3, 1),
 )
 
 
@@ -29,7 +37,7 @@
 
 def kernel(
     cur, near, proj, own, other, expand, out,
-    spec, low_rim, high_rim, near_re, near_im, near_neg, w_in, w_lev, w_out, far_raw, w_far, w_two, coef, part_in, near_sum, volt,
+    spec, low_rim, high_rim, near_re, near_im, w_in, w_lev, w_out, far_raw, w_far, w_two, coef, part_in, near_sum, volt,
     load_sem, spec_sem, fwd_send, fwd_recv, rim_send, rim_recv, lev_send, lev_recv, far_send, far_recv, ret_send, ret_recv, home_sem,
 ):
     box, f = lax.axis_index("box"), lax.axis_index("freq")
@@ -73,8 +81,11 @@
         load(source.at[:, 0, 0], w_lev.at[:, base : base + rank, 0:rank])
         load(source.at[:, 0, 1], w_lev.at[:, base : base + rank, rank : 2 * rank])
         load(source.at[:, 0, 0], w_lev.at[:, base + rank : base + 2 * rank, rank : 2 * rank])
-    load(near.at[0, 0], near_re)
-    load(near.at[0, 1], near_im)
+    width = near.shape[2]
+    load(near.at[0, 0], near_re.at[0:width])
+    load(near.at[0, 1], near_re.at[width : 2 * width])
+    load(near.at[0, 1], near_im.at[0:width])
+    load(near.at[0, 0], near_im.at[width : 2 * width])
     load(expand.at[0, 0], w_out.at[0:rank, 0:ports])
     load(expand.at[0, 1], w_out.at[0:rank, ports : 2 * ports])
     load(expand.at[0, 0], w_out.at[rank : 2 * rank, ports : 2 * ports])
@@ -196,22 +207,25 @@
             w_two[what, 0 : 4 * rank] = near_half.astype(jnp.bfloat16)
             w_two[what, 4 * rank : 8 * rank] = far_half.astype(jnp.bfloat16)
         elif what == "near":
-            for copy in loads[9:11]:
+            for copy in loads[9:13]:
                 copy.wait()
+
+            near_re[width : 2 * width] = -near_re[width : 2 * width]
 
             @pl.when(box == 0)
             def _():
-                near_re[0:HALO] = jnp.zeros((HALO, ports), jnp.bfloat16)
-                near_im[0:HALO] = jnp.zeros((HALO, ports), jnp.bfloat16)
+                for weights in (near_re, near_im):
+                    for top in (0, width):
+                        weights[top : top + HALO] = jnp.zeros((HALO, ports), jnp.bfloat16)
 
             @pl.when(box == boxes - 1)
             def _():
-                near_re[HALO + ports :] = jnp.zeros((HALO, ports), jnp.bfloat16)
-                near_im[HALO + ports :] = jnp.zeros((HALO, ports), jnp.bfloat16)
-
-            near_neg[...] = -near_im[...]
+                for weights in (near_re, near_im):
+                    for end in (width, 2 * width):
+                        weights[end - HALO : end] = jnp.zeros((HALO, ports), jnp.bfloat16)
+
         else:
-            for copy in loads[11:14]:
+            for copy in loads[13:16]:
                 copy.wait()
             w_out[rank : 2 * rank, 0:ports] = -w_out[0:rank, ports : 2 * ports]
 
@@ -252,24 +266,24 @@
         elif kind == "near":
             prepare("near")
             prepare("out")
-            pair = (2 * step[1], 2 * step[1] + 1)
-            for slot in pair:
-                for side in range(2):
-                    rim(slot, side).wait_recv()
-
-            def window(component):
-                bands = [low_rim[pair[0] : pair[1] + 1, component], spec[pair[0] : pair[1] + 1, component], high_rim[pair[0] : pair[1] + 1, component]]
-                return jnp.concatenate([band.reshape(2 * scen, band.shape[-1]) for band in bands], axis=-1)
-
-            real, imag = window(0), window(1)
-            near_sum[pair[0] : pair[1] + 1, :, 0:ports] = (dot(real, near_re[...]) + dot(imag, near_neg[...])).reshape(2, scen, ports)
-            near_sum[pair[0] : pair[1] + 1, :, ports:] = (dot(real, near_im[...]) + dot(imag, near_re[...])).reshape(2, scen, ports)
+            slot = step[1]
+            for side in range(2):
+                rim(slot, side).wait_recv()
+            bands = [band[slot, component] for component in range(2) for band in (low_rim, spec, high_rim)]
+            window = jnp.concatenate(bands, axis=-1)
+            for component, weights in enumerate((near_re, near_im)):
+                for left in range(0, ports, TILE):
+                    start = component * ports + left
+                    near_sum[slot, :, start : start + TILE] = dot(window, weights[:, left : left + TILE])
         else:
             slot, part = step[1:]
             lines = pl.ds(part * rows, rows)
-            total = (dot(coef[stages, slot, lines], w_out[...]) + near_sum[slot, lines]).astype(jnp.bfloat16)
-            volt[slot, 0, lines] = total[:, 0:ports]
-            volt[slot, 1, lines] = total[:, ports:]
+            final = coef[stages, slot, lines]
+            for component in range(2):
+                for left in range(0, ports, TILE):
+                    columns = slice(component * ports + left, component * ports + left + TILE)
+                    total = dot(final, w_out[:, columns]) + near_sum[slot, lines, columns]
+                    volt[slot, component, lines, left : left + TILE] = total.astype(jnp.bfloat16)
             if slot == 0:
                 home(part).start()
             else:
@@ -303,9 +317,8 @@
             pltpu.VMEM((4, 2, scen, ports), half),
             pltpu.VMEM((4, 2, scen, HALO), half),
             pltpu.VMEM((4, 2, scen, HALO), half),
-            pltpu.VMEM((width, ports), half),
-            pltpu.VMEM((width, ports), half),
-            pltpu.VMEM((width, ports), half),
+            pltpu.VMEM((2 * width, ports), half),
+            pltpu.VMEM((2 * width, ports), half),
             pltpu.VMEM((2 * ports, 2 * rank), half),
             pltpu.VMEM((levels, 4 * rank, 2 * rank), half),
             pltpu.VMEM((2 * rank, 2 * ports), half),
@@ -316,7 +329,7 @@
             pltpu.VMEM((stages, 3, 4, scen, 2 * rank), half),
             pltpu.VMEM((4, scen, 2 * ports), jnp.float32),
             pltpu.VMEM((4, 2, scen, ports), half),
-            pltpu.SemaphoreType.DMA((14,)),
+            pltpu.SemaphoreType.DMA((16,)),
             pltpu.SemaphoreType.DMA,
             pltpu.SemaphoreType.DMA((4,)),
             pltpu.SemaphoreType.DMA((4, SUB)),

time: 84 us -> 84.8 us (level)
  no operation moved by 1% of the time
where the time goes in v3:
time: 84.8 us; the launch traced here: 84 us
  Pallas kernels  80.3 us (95%)
  local copies, waits for them, and re-layouts  3.63 us (4%)
    pallas_call x1, Pallas kernels, local(): pl.pallas_call(kernel, out_shape=jax.ShapeDtypeStruct(spectra.shape, half...  80.3 us
    transpose x1, local copies, waits for them, and re-layouts, local(): return jnp.transpose(voltages, (0, 2, 1, 3))  2.05 us

profile of v3, /device:TPU:1, one launch (start us, length us, event | category | flops | bytes accessed | tf_op | source)
XLA Modules:
  0.0 84.0 jit_solution(1580660618697891005)
XLA Ops:
  0.0 0.0 copy-start.3
  0.0 0.0 copy-start.1
  0.0 0.0 copy-start
  0.0 0.0 copy-start.2
  0.0 1.5 %copy.10 = bf16[4,128,2,512]{3,1,2,0:T(8,128)(2,1)S(1)} copy(bf16[4,128,2,512]{3,2,1,0:T(2,128)(2,1)} %param.6) | data formatting | bytes 2097152 | tf_op args[0]
  1.5 0.0 copy-done.3
  1.5 0.0 copy-done.1
  1.6 0.0 copy-done
  1.6 0.1 copy-done.2
  1.6 80.3 %shard_map.64 = bf16[4,2,128,512]{3,2,1,0:T(8,128)(2,1)S(1)} custom-call(bf16[4,2,128,512]{3,2,1,0:T(8,128)(2,1)S(1)} %bitcast.5, bf16[1,2,768,512]{3,2,1,0:T(8,128)(2,1)} %near.1, bf16[1,2,512,128]{3,2,1,0:T(8,128)(2,1)S(1)} %copy-done.2, bf16[7,1,2,128,128]{4,3,2,1,0:T(8,128)(2,1)S(1)} %copy-done, bf16[7,1,2,128,128]{4,3,2,1,0:T(8,128)(2,1)S(1)} %copy-done.1, ...), custom_call_target="tpu_custom_call" | custom-call | flops 3221225472 | bytes 6291456 | tf_op jit(solution)/shard_map/pallas_call | solution.py:311
  82.0 2.0 %copy.8 = bf16[4,128,2,512]{3,2,1,0:T(2,128)(2,1)} copy(bf16[4,128,2,512]{3,1,2,0:T(8,128)(2,1)S(1)} %bitcast.4) | data formatting | bytes 2097152 | tf_op jit(solution)/shard_map/transpose | solution.py:349
Async XLA Ops:
  0.0 1.5 %copy-start.3 = (bf16[1,2,128,512]{3,2,1,0:T(8,128)(2,1)S(1)}, bf16[1,2,128,512]{3,2,1,0:T(8,128)(2,1)}, u32[]{:S(2)}) copy-start(bf16[1,2,128,512]{3,2,1,0:T(8,128)(2,1)} %expand.1) | copy-start | bytes 786436
  0.0 1.5 %copy-start.1 = (bf16[7,1,2,128,128]{4,3,2,1,0:T(8,128)(2,1)S(1)}, bf16[7,1,2,128,128]{4,3,2,1,0:T(8,128)(2,1)}, u32[]{:S(2)}) copy-start(bf16[7,1,2,128,128]{4,3,2,1,0:T(8,128)(2,1)} %other.1) | copy-start | bytes 1376260
  0.0 1.6 %copy-start = (bf16[7,1,2,128,128]{4,3,2,1,0:T(8,128)(2,1)S(1)}, bf16[7,1,2,128,128]{4,3,2,1,0:T(8,128)(2,1)}, u32[]{:S(2)}) copy-start(bf16[7,1,2,128,128]{4,3,2,1,0:T(8,128)(2,1)} %own.1) | copy-start | bytes 1376260
  0.0 1.6 %copy-start.2 = (bf16[1,2,512,128]{3,2,1,0:T(8,128)(2,1)S(1)}, bf16[1,2,512,128]{3,2,1,0:T(8,128)(2,1)}, u32[]{:S(2)}) copy-start(bf16[1,2,512,128]{3,2,1,0:T(8,128)(2,1)} %proj.1) | copy-start | bytes 786436

commit v4 on v3

--- a/solution.py
+++ b/solution.py
@@ -9,25 +9,18 @@
 
 HALO = 128
 TILE = 256
-SUB = 2
+SUB = 1
 MESH = pl.DeviceIdType.MESH
 STAGES = ((0, 1), (2,), (3, 4), (5, 6))
 STEPS = (
-    ("project", 0, 0), ("project", 0, 1), ("rims", 0), ("project", 1, 0),
-    ("onward",), ("project", 1, 1), ("level", 0, 0, 0), ("project", 2, 0),
-    ("rims", 1), ("level", 0, 0, 1), ("level", 0, 1, 0), ("level", 1, 0, 0),
-    ("project", 3, 0), ("level", 1, 0, 1), ("project", 2, 1), ("level", 0, 1, 1),
-    ("near", 0), ("rims", 2), ("level", 1, 1, 0), ("near", 1),
-    ("project", 3, 1), ("level", 0, 2, 0), ("level", 0, 3, 0), ("rims", 3),
-    ("level", 0, 2, 1), ("level", 2, 0, 0), ("level", 1, 1, 1), ("near", 2),
-    ("level", 0, 3, 1), ("level", 2, 0, 1), ("level", 1, 2, 0), ("level", 2, 1, 0),
-    ("level", 3, 0, 0), ("level", 1, 3, 0), ("level", 2, 1, 1), ("finish", 0, 0),
-    ("level", 1, 2, 1), ("level", 2, 2, 0), ("level", 3, 1, 0), ("level", 2, 3, 0),
-    ("finish", 1, 0), ("level", 1, 3, 1), ("level", 2, 2, 1), ("level", 3, 0, 1),
-    ("level", 3, 2, 0), ("finish", 2, 0), ("level", 3, 1, 1), ("level", 2, 3, 1),
-    ("finish", 0, 1), ("level", 3, 3, 0), ("level", 3, 2, 1), ("finish", 2, 1),
-    ("finish", 1, 1), ("near", 3), ("finish", 3, 0), ("level", 3, 3, 1),
-    ("finish", 3, 1),
+    ("project", 0, 0), ("project", 1, 0), ("level", 0, 0, 0), ("rims", 0),
+    ("level", 1, 0, 0), ("rims", 1), ("level", 0, 1, 0), ("project", 2, 0),
+    ("near", 1), ("project", 3, 0), ("factors",), ("level", 0, 2, 0), ("rims", 2),
+    ("rims", 3), ("level", 1, 1, 0), ("level", 2, 0, 0), ("level", 0, 3, 0),
+    ("near", 0), ("near", 3), ("level", 1, 2, 0), ("level", 2, 1, 0),
+    ("level", 3, 0, 0), ("finish", 0, 0), ("level", 1, 3, 0), ("level", 2, 2, 0),
+    ("near", 2), ("level", 2, 3, 0), ("level", 3, 2, 0), ("finish", 2, 0),
+    ("level", 3, 1, 0), ("level", 3, 3, 0), ("finish", 3, 0), ("finish", 1, 0),
 )
 
 
@@ -170,7 +163,7 @@
         forward(slot, 0).start()
     for part in range(SUB):
         forward(1, part).start()
-    for place in range(len(twos)):
+    for place in range(len(twos) - 1):
         for copy in factors(place):
             copy.start()
 
@@ -245,6 +238,9 @@
             for part in range(1, SUB):
                 for slot in (2, 3):
                     forward(slot, part).start()
+        elif kind == "factors":
+            for copy in factors(len(twos) - 1):
+                copy.start()
         elif kind == "rims":
             for side in range(2):
                 rim(step[1], side).start()

time: 84.8 us -> 82.6 us (0.974)
  Pallas kernels: 80.3 us -> 77.7 us
    pallas_call x1, Pallas kernels: 80.3 us -> 77.7 us  [local(): pl.pallas_call(kernel, out_shape=jax.ShapeDtypeStruct(spectra.shape, half...]
where the time goes in v4:
time: 82.6 us; the launch traced here: 81.4 us
  Pallas kernels  77.7 us (94%)
  local copies, waits for them, and re-layouts  3.63 us (4%)
    pallas_call x1, Pallas kernels, local(): pl.pallas_call(kernel, out_shape=jax.ShapeDtypeStruct(spectra.shape, half...  77.7 us
    transpose x1, local copies, waits for them, and re-layouts, local(): return jnp.transpose(voltages, (0, 2, 1, 3))  2.05 us

profile of v4, /device:TPU:1, one launch (start us, length us, event | category | flops | bytes accessed | tf_op | source)
XLA Modules:
  0.0 81.4 jit_solution(17394905509239168374)
XLA Ops:
  0.0 0.0 copy-start.3
  0.0 0.0 copy-start.1
  0.0 0.0 copy-start
  0.0 0.0 copy-start.2
  0.0 1.5 %copy.10 = bf16[4,128,2,512]{3,1,2,0:T(8,128)(2,1)S(1)} copy(bf16[4,128,2,512]{3,2,1,0:T(2,128)(2,1)} %param.6) | data formatting | bytes 2097152 | tf_op args[0]
  1.5 0.0 copy-done.3
  1.5 0.0 copy-done.1
  1.6 0.0 copy-done
  1.6 0.1 copy-done.2
  1.6 77.7 %shard_map.64 = bf16[4,2,128,512]{3,2,1,0:T(8,128)(2,1)S(1)} custom-call(bf16[4,2,128,512]{3,2,1,0:T(8,128)(2,1)S(1)} %bitcast.5, bf16[1,2,768,512]{3,2,1,0:T(8,128)(2,1)} %near.1, bf16[1,2,512,128]{3,2,1,0:T(8,128)(2,1)S(1)} %copy-done.2, bf16[7,1,2,128,128]{4,3,2,1,0:T(8,128)(2,1)S(1)} %copy-done, bf16[7,1,2,128,128]{4,3,2,1,0:T(8,128)(2,1)S(1)} %copy-done.1, ...), custom_call_target="tpu_custom_call" | custom-call | flops 3221225472 | bytes 6291456 | tf_op jit(solution)/shard_map/pallas_call | solution.py:307
  79.3 2.0 %copy.8 = bf16[4,128,2,512]{3,2,1,0:T(2,128)(2,1)} copy(bf16[4,128,2,512]{3,1,2,0:T(8,128)(2,1)S(1)} %bitcast.4) | data formatting | bytes 2097152 | tf_op jit(solution)/shard_map/transpose | solution.py:345
Async XLA Ops:
  0.0 1.5 %copy-start.3 = (bf16[1,2,128,512]{3,2,1,0:T(8,128)(2,1)S(1)}, bf16[1,2,128,512]{3,2,1,0:T(8,128)(2,1)}, u32[]{:S(2)}) copy-start(bf16[1,2,128,512]{3,2,1,0:T(8,128)(2,1)} %expand.1) | copy-start | bytes 786436
  0.0 1.5 %copy-start.1 = (bf16[7,1,2,128,128]{4,3,2,1,0:T(8,128)(2,1)S(1)}, bf16[7,1,2,128,128]{4,3,2,1,0:T(8,128)(2,1)}, u32[]{:S(2)}) copy-start(bf16[7,1,2,128,128]{4,3,2,1,0:T(8,128)(2,1)} %other.1) | copy-start | bytes 1376260
  0.0 1.6 %copy-start = (bf16[7,1,2,128,128]{4,3,2,1,0:T(8,128)(2,1)S(1)}, bf16[7,1,2,128,128]{4,3,2,1,0:T(8,128)(2,1)}, u32[]{:S(2)}) copy-start(bf16[7,1,2,128,128]{4,3,2,1,0:T(8,128)(2,1)} %own.1) | copy-start | bytes 1376260
  0.0 1.6 %copy-start.2 = (bf16[1,2,512,128]{3,2,1,0:T(8,128)(2,1)S(1)}, bf16[1,2,512,128]{3,2,1,0:T(8,128)(2,1)}, u32[]{:S(2)}) copy-start(bf16[1,2,512,128]{3,2,1,0:T(8,128)(2,1)} %proj.1) | copy-start | bytes 786436

commit v5 on v4

--- a/solution.py
+++ b/solution.py
@@ -13,7 +13,7 @@
 MESH = pl.DeviceIdType.MESH
 STAGES = ((0, 1), (2,), (3, 4), (5, 6))
 STEPS = (
-    ("project", 0, 0), ("project", 1, 0), ("level", 0, 0, 0), ("rims", 0),
+    ("project", 0, 0), ("project", 1, 0), ("onward",), ("level", 0, 0, 0), ("rims", 0),
     ("level", 1, 0, 0), ("rims", 1), ("level", 0, 1, 0), ("project", 2, 0),
     ("near", 1), ("project", 3, 0), ("factors",), ("level", 0, 2, 0), ("rims", 2),
     ("rims", 3), ("level", 1, 1, 0), ("level", 2, 0, 0), ("level", 0, 3, 0),
@@ -159,8 +159,7 @@
         lines = pl.ds(part * rows, rows)
         return pltpu.make_async_copy(volt.at[0, :, lines], out.at[f, :, lines], home_sem)
 
-    for slot in (2, 3):
-        forward(slot, 0).start()
+    forward(2, 0).start()
     for part in range(SUB):
         forward(1, part).start()
     for place in range(len(twos) - 1):
@@ -235,9 +234,7 @@
                 copy.start()
             prepare("level")
         elif kind == "onward":
-            for part in range(1, SUB):
-                for slot in (2, 3):
-                    forward(slot, part).start()
+            forward(3, 0).start()
         elif kind == "factors":
             for copy in factors(len(twos) - 1):
                 copy.start()

time: 82.6 us -> 82.6 us (level)
  no operation moved by 1% of the time
where the time goes in v5:
time: 82.6 us; the launch traced here: 81.4 us
  Pallas kernels  77.7 us (94%)
  local copies, waits for them, and re-layouts  3.63 us (4%)
    pallas_call x1, Pallas kernels, local(): pl.pallas_call(kernel, out_shape=jax.ShapeDtypeStruct(spectra.shape, half...  77.7 us
    transpose x1, local copies, waits for them, and re-layouts, local(): return jnp.transpose(voltages, (0, 2, 1, 3))  2.05 us

profile of v5, /device:TPU:1, one launch (start us, length us, event | category | flops | bytes accessed | tf_op | source)
XLA Modules:
  0.0 81.4 jit_solution(15104745417933213489)
XLA Ops:
  0.0 0.0 copy-start.3
  0.0 0.0 copy-start.1
  0.0 0.0 copy-start
  0.0 0.0 copy-start.2
  0.0 1.5 %copy.10 = bf16[4,128,2,512]{3,1,2,0:T(8,128)(2,1)S(1)} copy(bf16[4,128,2,512]{3,2,1,0:T(2,128)(2,1)} %param.6) | data formatting | bytes 2097152 | tf_op args[0]
  1.5 0.0 copy-done.3
  1.5 0.0 copy-done.1
  1.6 0.0 copy-done
  1.6 0.1 copy-done.2
  1.6 77.7 %shard_map.64 = bf16[4,2,128,512]{3,2,1,0:T(8,128)(2,1)S(1)} custom-call(bf16[4,2,128,512]{3,2,1,0:T(8,128)(2,1)S(1)} %bitcast.5, bf16[1,2,768,512]{3,2,1,0:T(8,128)(2,1)} %near.1, bf16[1,2,512,128]{3,2,1,0:T(8,128)(2,1)S(1)} %copy-done.2, bf16[7,1,2,128,128]{4,3,2,1,0:T(8,128)(2,1)S(1)} %copy-done, bf16[7,1,2,128,128]{4,3,2,1,0:T(8,128)(2,1)S(1)} %copy-done.1, ...), custom_call_target="tpu_custom_call" | custom-call | flops 3221225472 | bytes 6291456 | tf_op jit(solution)/shard_map/pallas_call | solution.py:304
  79.3 2.0 %copy.8 = bf16[4,128,2,512]{3,2,1,0:T(2,128)(2,1)} copy(bf16[4,128,2,512]{3,1,2,0:T(8,128)(2,1)S(1)} %bitcast.4) | data formatting | bytes 2097152 | tf_op jit(solution)/shard_map/transpose | solution.py:342
Async XLA Ops:
  0.0 1.5 %copy-start.3 = (bf16[1,2,128,512]{3,2,1,0:T(8,128)(2,1)S(1)}, bf16[1,2,128,512]{3,2,1,0:T(8,128)(2,1)}, u32[]{:S(2)}) copy-start(bf16[1,2,128,512]{3,2,1,0:T(8,128)(2,1)} %expand.1) | copy-start | bytes 786436
  0.0 1.5 %copy-start.1 = (bf16[7,1,2,128,128]{4,3,2,1,0:T(8,128)(2,1)S(1)}, bf16[7,1,2,128,128]{4,3,2,1,0:T(8,128)(2,1)}, u32[]{:S(2)}) copy-start(bf16[7,1,2,128,128]{4,3,2,1,0:T(8,128)(2,1)} %other.1) | copy-start | bytes 1376260
  0.0 1.6 %copy-start = (bf16[7,1,2,128,128]{4,3,2,1,0:T(8,128)(2,1)S(1)}, bf16[7,1,2,128,128]{4,3,2,1,0:T(8,128)(2,1)}, u32[]{:S(2)}) copy-start(bf16[7,1,2,128,128]{4,3,2,1,0:T(8,128)(2,1)} %own.1) | copy-start | bytes 1376260
  0.0 1.6 %copy-start.2 = (bf16[1,2,512,128]{3,2,1,0:T(8,128)(2,1)S(1)}, bf16[1,2,512,128]{3,2,1,0:T(8,128)(2,1)}, u32[]{:S(2)}) copy-start(bf16[1,2,512,128]{3,2,1,0:T(8,128)(2,1)} %proj.1) | copy-start | bytes 786436
